TPU v7x, 32 devices: a whole 2x2x4 slice. The times are simulated.
32 devices in a mesh: dp: 16 (over z, x, core), blk: 2 (over y).
Axes of the slice: x: 2, y: 2, z: 4, core: 2. Of those that a mesh axis runs over, the one named last changes fastest.
Arguments:
- waveform: bfloat16 [512, 330], P(('dp', 'blk')), may hold values from -6 to 6
- length_bin: int32 [512], P(('dp', 'blk')), may hold values from 1 to 4
- packing: int32 [32, 16], P(('dp', 'blk')), may hold values from 0 to 15, each once within a row
- cotangent: bfloat16 [512, 32, 512], P(('dp', 'blk')), may hold values from -6 to 6
- conv_one: bfloat16 [10, 512], replicated, may hold values from -2 to 2
- bias_one: float32 [512], replicated, may hold values from -6 to 6
- gain_one: float32 [512], replicated, may hold values from 2 to 8
- shift_one: float32 [512], replicated, may hold values from -12 to 12
- conv_two: bfloat16 [1536, 512], replicated, may hold values from -0.15625 to 0.15625
- bias_two: float32 [512], replicated, may hold values from -6 to 6
- gain_two: float32 [512], replicated, may hold values from 0.5 to 1.5
- shift_two: float32 [512], replicated, may hold values from -3 to 3
Outputs:
- grad_conv_two: float32 [1536, 512], P('dp')
- grad_small: float32 [16, 512], replicated
All inputs are finite; a program needn't handle non-finite values.
Results may differ from a plain program's by a relative error of at most 0.0046.
Values may be sent and summed in bfloat16 or wider, within the bound.
No kernel may reach another device: no remote copies, remote signals or barrier semaphores. Data moves between devices by JAX's collectives and lax.ppermute only.
A program may use at most 64 MiB of HBM per device.

v0:
```python
import jax
import jax.numpy as jnp
from jax import lax
from jax.sharding import PartitionSpec as P

NB = 4
GROUP = 8


def norm_act(z, gain, shift):
    mean = jnp.mean(z, axis=-1, keepdims=True)
    cent = z - mean
    var = jnp.mean(cent * cent, axis=-1, keepdims=True)
    rstd = lax.rsqrt(var + 1e-05)
    normed = cent * rstd
    return (normed * gain + shift, normed, rstd)


def gelu_exact(act):
    return 0.5 * act * (1.0 + lax.erf(act * 0.7071067811865476))


def norm_back(grad_out, act, normed, rstd, gain):
    cdf = 0.5 * (1.0 + lax.erf(act * 0.7071067811865476))
    pdf = jnp.exp(-0.5 * act * act) * 0.3989422804014327
    grad_act = grad_out * (cdf + act * pdf)
    grad_gain = jnp.sum(grad_act * normed, axis=0)
    grad_shift = jnp.sum(grad_act, axis=0)
    grad_norm = grad_act * gain
    inner = grad_norm - jnp.mean(grad_norm, axis=-1, keepdims=True)
    inner = inner - normed * jnp.mean(grad_norm * normed, axis=-1, keepdims=True)
    return (rstd * inner, grad_gain, grad_shift)


def pass_group(
    wave,
    bins,
    cot,
    conv_one,
    bias_one,
    gain_one,
    shift_one,
    conv_two,
    bias_two,
    gain_two,
    shift_two,
):
    count = wave.shape[0]
    frames_two = cot.shape[1]
    width = cot.shape[2]
    frames_one = 2 * frames_two + 1
    split = wave.reshape(count, frames_one + 1, 5)
    cols_one = jnp.concatenate([split[:, :-1], split[:, 1:]], axis=-1).reshape(
        count * frames_one, 10
    )
    z_one = jnp.dot(cols_one, conv_one, preferred_element_type=jnp.float32) + bias_one
    act_one, normed_one, rstd_one = norm_act(z_one, gain_one, shift_one)
    hidden = gelu_exact(act_one).astype(jnp.bfloat16).reshape(count, frames_one, width)
    cols_two = jnp.concatenate(
        [hidden[:, : 2 * frames_two].reshape(count, frames_two, 2 * width), hidden[:, 2::2]],
        axis=-1,
    )
    cols_two = cols_two.reshape(count * frames_two, 3 * width)
    z_two = jnp.dot(cols_two, conv_two, preferred_element_type=jnp.float32) + bias_two
    act_two, normed_two, rstd_two = norm_act(z_two, gain_two, shift_two)
    limit = bins * frames_two // NB
    valid = (jnp.arange(frames_two, dtype=jnp.int32)[None, :] < limit[:, None]).astype(jnp.float32)
    grad_out = (cot.astype(jnp.float32) * valid[:, :, None]).reshape(count * frames_two, width)
    dz_two, dgain_two, dshift_two = norm_back(grad_out, act_two, normed_two, rstd_two, gain_two)
    dbias_two = jnp.sum(dz_two, axis=0)
    dz_two_b = dz_two.astype(jnp.bfloat16)
    dcols = jnp.dot(dz_two_b, conv_two.T, preferred_element_type=jnp.float32).reshape(
        count, frames_two, 3 * width
    )
    part_a = dcols[:, :, : 2 * width].reshape(count, 2 * frames_two, width)
    part_b = dcols[:, :, 2 * width :]
    spread = jnp.stack([part_b, jnp.zeros_like(part_b)], axis=2).reshape(
        count, 2 * frames_two, width
    )
    zero_one = jnp.zeros((count, 1, width), jnp.float32)
    zero_two = jnp.zeros((count, 2, width), jnp.float32)
    dhidden = jnp.concatenate([part_a, zero_one], axis=1) + jnp.concatenate(
        [zero_two, spread[:, : 2 * frames_two - 1]], axis=1
    )
    dz_one, dgain_one, dshift_one = norm_back(
        dhidden.reshape(count * frames_one, width), act_one, normed_one, rstd_one, gain_one
    )
    dbias_one = jnp.sum(dz_one, axis=0)
    dconv_one = jnp.dot(cols_one.T, dz_one.astype(jnp.bfloat16), preferred_element_type=jnp.float32)
    small = jnp.concatenate(
        [
            dconv_one,
            jnp.stack([dbias_one, dgain_one, dshift_one, dbias_two, dgain_two, dshift_two]),
        ],
        axis=0,
    )
    return (cols_two, dz_two_b, small)


def per_device(
    waveform,
    length_bin,
    packing,
    cotangent,
    conv_one,
    bias_one,
    gain_one,
    shift_one,
    conv_two,
    bias_two,
    gain_two,
    shift_two,
):
    order_list = packing[0]
    sent_wave = waveform[order_list]
    sent_bins = length_bin[order_list]
    wave, bins = (
        lax.all_to_all(sent_wave, "dp", split_axis=0, concat_axis=0, tiled=True),
        lax.all_to_all(sent_bins, "dp", split_axis=0, concat_axis=0, tiled=True),
    )
    count = wave.shape[0]
    record = wave.shape[1]
    frames_two = cotangent.shape[1]
    width = cotangent.shape[2]
    groups = count // GROUP
    xs = (
        wave.reshape(groups, GROUP, record),
        bins.reshape(groups, GROUP),
        cotangent.reshape(groups, GROUP, frames_two, width),
    )

    def step(small_sum, item):
        cols_two, dz_two_b, small = pass_group(
            item[0],
            item[1],
            item[2],
            conv_one,
            bias_one,
            gain_one,
            shift_one,
            conv_two,
            bias_two,
            gain_two,
            shift_two,
        )
        return (small_sum + small, (cols_two, dz_two_b))

    small_local, stacked = lax.scan(step, jnp.zeros((16, width), jnp.float32), xs)
    cols_all = stacked[0].reshape(count * frames_two, 3 * width)
    dz_all = stacked[1].reshape(count * frames_two, width)
    term = lax.dot_general(
        cols_all, dz_all, (((0,), (0,)), ((), ())), preferred_element_type=jnp.float32
    )
    whole = lax.psum(term, "blk")
    share = lax.psum_scatter(whole, "dp", scatter_dimension=0, tiled=True)
    small_total = lax.psum(small_local, ("dp", "blk"))
    return (share, small_total)


def solution(mesh):
    return jax.shard_map(
        per_device,
        mesh=mesh,
        in_specs=(
            P(("dp", "blk"), None),
            P(("dp", "blk")),
            P(("dp", "blk"), None),
            P(("dp", "blk"), None, None),
            P(),
            P(),
            P(),
            P(),
            P(),
            P(),
            P(),
            P(),
        ),
        out_specs=(P("dp", None), P()),
        check_vma=False,
    )
```

profile of v0, /device:TPU:0, one launch (start us, length us, event | category | flops | bytes accessed | tf_op | source)
XLA Modules:
  0.0 192.3 jit_solution(11816954975854196462)
XLA Ops:
  7.9 1.3 gather_fusion.1
  9.9 7.4 %all-to-all-start.1 = ((s32[16,1,1]{2,1,0:T(1,128)}), s32[16,1,1]{2,1,0:T(1,128)S(1)}, u32[]{:S(2)}, u32[]{:S(2)}) async-start(s32[16,1,1]{2,1,0:T(1,128)} %copy.29), calls=%async_computation.1 | async-start | bytes 16384 | tf_op jit(solution)/shard_map/all_to_all | solution.py:119
  19.7 3.9 %all-to-all-done.1 = s32[16,1,1]{2,1,0:T(1,128)S(1)} async-done(((s32[16,1,1]{2,1,0:T(1,128)}), s32[16,1,1]{2,1,0:T(1,128)S(1)}, u32[]{:S(2)}, u32[]{:S(2)}) %all-to-all-start.1) | async-done | bytes 96 | tf_op jit(solution)/shard_map/all_to_all | solution.py:119
  23.6 3.5 %all-to-all-start = ((bf16[16,2,165]{2,1,0:T(2,128)(2,1)}), bf16[16,2,165]{2,1,0:T(2,128)(2,1)S(1)}, u32[]{:S(2)}, u32[]{:S(2)}) async-start(bf16[16,2,165]{2,1,0:T(2,128)(2,1)} %reshape.260), calls=%async_computation | async-start | bytes 32768 | tf_op jit(solution)/shard_map/all_to_all | solution.py:118
  28.2 5.3 %all-to-all-done = bf16[16,2,165]{2,1,0:T(2,128)(2,1)S(1)} async-done(((bf16[16,2,165]{2,1,0:T(2,128)(2,1)}), bf16[16,2,165]{2,1,0:T(2,128)(2,1)S(1)}, u32[]{:S(2)}, u32[]{:S(2)}) %all-to-all-start) | async-done | bytes 10592 | tf_op jit(solution)/shard_map/all_to_all | solution.py:118
  34.2 41.1 %while.17 = (s32[]{:T(128)}, f32[16,512]{1,0:T(8,128)}, bf16[2,256,1536]{2,1,0:T(8,128)(2,1)}, bf16[2,256,512]{2,1,0:T(8,128)(2,1)}, bf16[2,8,330]{2,1,0:T(8,128...) while((s32[]{:T(128)}, f32[16,512]{1,0:T(8,128)}, ...), condition=%wide.region_15.16_spmd.clone, body=%wide.region_0.15_spmd.clone.sunk | while | flops 835685888 | bytes 56027588 | solution.py:148
  39.0 2.1 %fusion.59 = (f32[256]{0:T(256)S(1)}, f32[256,512]{1,0:T(8,128)S(1)}) fusion(f32[512]{0:T(512)S(1)} %copy-done.11, bf16[1536,512]{1,0:T(8,128)(2,1)} %get-tuple-element.475, bf16[256,512]{1,0:T(8,128)(2,1)S(1)} %bitcast.85, bf16[256,1024]{1,0:T(8,128)(2,1)S(1)} %concatenate.58), kind=kOutput, calls=%fused_computation.73.clone.1 | convolution fusion | flops 404487936 | bytes 2886656 | tf_op jit(solution)/shard_map/while/body/eval_jaxpr/dot_general | solution.py:64
  43.3 0.9 maximum_dynamic-update-slice_fusion.2
  45.6 0.8 slice_bitcast_fusion.2
  46.7 1.6 copy.42
  48.6 1.7 reshape.273
  50.4 1.5 pad_add_fusion.2
  52.0 1.1 multiply_reduce_fusion.15
  59.2 2.1 %fusion.59 = (f32[256]{0:T(256)S(1)}, f32[256,512]{1,0:T(8,128)S(1)}) fusion(f32[512]{0:T(512)S(1)} %copy-done.11, bf16[1536,512]{1,0:T(8,128)(2,1)} %get-tuple-element.475, bf16[256,512]{1,0:T(8,128)(2,1)S(1)} %bitcast.85, bf16[256,1024]{1,0:T(8,128)(2,1)S(1)} %concatenate.58), kind=kOutput, calls=%fused_computation.73.clone.1 | convolution fusion | flops 404487936 | bytes 2886656 | tf_op jit(solution)/shard_map/while/body/eval_jaxpr/dot_general | solution.py:64
  63.5 0.9 maximum_dynamic-update-slice_fusion.2
  66.9 1.6 copy.42
  68.8 1.7 reshape.273
  70.6 1.5 pad_add_fusion.2
  72.2 1.1 multiply_reduce_fusion.15
  74.0 1.4 select_add_fusion.2
  75.4 4.2 %convolution_bitcast_fusion = f32[1536,512]{1,0:T(8,128)} fusion(bf16[2,256,1536]{2,1,0:T(8,128)(2,1)} %get-tuple-element.190, bf16[2,256,512]{2,1,0:T(8,128)(2,1)} %get-tuple-element.191), kind=kOutput, calls=%fused_computation.65 | convolution fusion | flops 805306368 | bytes 5242880 | tf_op jit(solution)/shard_map/dot_general | solution.py:151
  79.6 63.6 %reduce-scatter.2.cloned.1.call-done = f32[96,512]{1,0:T(8,128)} async-done(((f32[1536,512]{1,0:T(8,128)}), f32[96,512]{1,0:T(8,128)}) %reduce-scatter.2.cloned.1.call-update) | async-done | bytes 196624 | tf_op jit(solution)/shard_map/reduce_scatter | solution.py:155
  143.3 40.6 %psum.15 = f32[16,512]{1,0:T(8,128)} all-reduce(f32[16,512]{1,0:T(8,128)} %get-tuple-element.192), channel_id=1, replica_groups=mesh['dp'=16,'blk'=2] {'dp','blk'}, use_global_device_ids=true, to_apply=%region_18.19 | all-reduce | flops 8192 | bytes 65536 | tf_op jit(solution)/shard_map/psum | solution.py:156
  183.9 1.6 copy.58
  (143 shorter events, 26.2 us)
Async XLA Ops:
  7.2 10.1 %copy-start = (bf16[16,330]{1,0:T(8,128)(2,1)S(1)}, bf16[16,330]{1,0:T(8,128)(2,1)}, u32[]{:S(2)}) copy-start(bf16[16,330]{1,0:T(8,128)(2,1)} %param.14) | copy-start | bytes 31684
  9.9 13.7 %all-to-all-start.1 = ((s32[16,1,1]{2,1,0:T(1,128)}), s32[16,1,1]{2,1,0:T(1,128)S(1)}, u32[]{:S(2)}, u32[]{:S(2)}) async-start(s32[16,1,1]{2,1,0:T(1,128)} %copy.29), calls=%async_computation.1 | async-start | bytes 16384 | tf_op jit(solution)/shard_map/all_to_all | solution.py:119
  23.6 10.0 %all-to-all-start = ((bf16[16,2,165]{2,1,0:T(2,128)(2,1)}), bf16[16,2,165]{2,1,0:T(2,128)(2,1)S(1)}, u32[]{:S(2)}, u32[]{:S(2)}) async-start(bf16[16,2,165]{2,1,0:T(2,128)(2,1)} %reshape.260), calls=%async_computation | async-start | bytes 32768 | tf_op jit(solution)/shard_map/all_to_all | solution.py:118
  27.1 116.2 %reduce-scatter.2.cloned.1.call-start = ((), (), s32[]{:S(2)}) async-start(), calls=%async_computation.3 | async-start | bytes 3342336 | tf_op jit(solution)/shard_map/reduce_scatter | solution.py:155
  34.2 2.3 %copy-start.2 = (bf16[2,8,32,512]{3,2,1,0:T(8,128)(2,1)S(1)}, bf16[2,8,32,512]{3,2,1,0:T(8,128)(2,1)}, u32[]{:S(2)}) copy-start(bf16[2,8,32,512]{3,2,1,0:T(8,128)(2,1)} %get-tuple-element.477) | copy-start | bytes 1572868 | tf_op jit(solution)/shard_map/while
  34.2 2.3 %copy-start.4 = (bf16[10,512]{1,0:T(8,128)(2,1)S(1)}, bf16[10,512]{1,0:T(8,128)(2,1)}, u32[]{:S(2)}) copy-start(bf16[10,512]{1,0:T(8,128)(2,1)} %get-tuple-element.471) | copy-start | bytes 30724 | tf_op jit(solution)/shard_map/while
  34.2 2.3 %copy-start.7 = (f32[512]{0:T(512)S(1)}, f32[512]{0:T(512)}, u32[]{:S(2)}) copy-start(f32[512]{0:T(512)} %get-tuple-element.472) | copy-start | bytes 6148 | tf_op jit(solution)/shard_map/while
  36.5 0.8 copy-start.3
  36.5 0.8 copy-start.5
  39.0 2.3 %copy-start.6 = (f32[512]{0:T(512)S(1)}, f32[512]{0:T(512)}, u32[]{:S(2)}) copy-start(f32[512]{0:T(512)} %get-tuple-element.479) | copy-start | bytes 6148 | tf_op jit(solution)/shard_map/while
  39.0 2.3 %copy-start.8 = (f32[512]{0:T(512)S(1)}, f32[512]{0:T(512)}, u32[]{:S(2)}) copy-start(f32[512]{0:T(512)} %get-tuple-element.480) | copy-start | bytes 6148 | tf_op jit(solution)/shard_map/while
  41.1 1.0 copy-start.9
  42.4 0.8 copy-start.10
  43.3 1.7 copy-start.1
  54.4 2.3 %copy-start.2 = (bf16[2,8,32,512]{3,2,1,0:T(8,128)(2,1)S(1)}, bf16[2,8,32,512]{3,2,1,0:T(8,128)(2,1)}, u32[]{:S(2)}) copy-start(bf16[2,8,32,512]{3,2,1,0:T(8,128)(2,1)} %get-tuple-element.477) | copy-start | bytes 1572868 | tf_op jit(solution)/shard_map/while
  54.4 2.3 %copy-start.4 = (bf16[10,512]{1,0:T(8,128)(2,1)S(1)}, bf16[10,512]{1,0:T(8,128)(2,1)}, u32[]{:S(2)}) copy-start(bf16[10,512]{1,0:T(8,128)(2,1)} %get-tuple-element.471) | copy-start | bytes 30724 | tf_op jit(solution)/shard_map/while
  54.4 2.3 %copy-start.7 = (f32[512]{0:T(512)S(1)}, f32[512]{0:T(512)}, u32[]{:S(2)}) copy-start(f32[512]{0:T(512)} %get-tuple-element.472) | copy-start | bytes 6148 | tf_op jit(solution)/shard_map/while
  56.7 0.8 copy-start.3
  59.2 2.3 %copy-start.6 = (f32[512]{0:T(512)S(1)}, f32[512]{0:T(512)}, u32[]{:S(2)}) copy-start(f32[512]{0:T(512)} %get-tuple-element.479) | copy-start | bytes 6148 | tf_op jit(solution)/shard_map/while
  59.2 2.3 %copy-start.8 = (f32[512]{0:T(512)S(1)}, f32[512]{0:T(512)}, u32[]{:S(2)}) copy-start(f32[512]{0:T(512)} %get-tuple-element.480) | copy-start | bytes 6148 | tf_op jit(solution)/shard_map/while
  61.3 1.0 copy-start.9
  62.6 0.8 copy-start.10
  63.5 1.7 copy-start.1
  79.6 104.3 %all-reduce.5.cloned.1.call-start = ((), (), s32[]{:S(2)}) async-start(), calls=%async_computation.4 | async-start | bytes 393216 | tf_op jit(solution)/shard_map/psum | solution.py:154
  (3 other events, 2.1 us)
Sparse Core Ops, SparseCore 0:
  79.7 63.4 reduce-scatter.1
  145.5 21.4 all-reduce.4
where the time goes:
time: 193 us; the launch traced here: 192 us
  waiting for transfers between devices  72.8 us (38%)
  blocking collectives  40.6 us (21%)
  local copies, waits for them, and re-layouts  25.6 us (13%)
  other arithmetic  16.9 us (9%)
  between operations  14.1 us (7%)
  starting transfers between devices  10.9 us (6%)
  matrix products  10.8 us (6%)
    reduce_scatter x1, waiting for transfers between devices, per_device(): share = lax.psum_scatter(whole, 'dp', scatter_dimension=0, tiled=True)  63.6 us
    psum x1, blocking collectives, per_device(): small_total = lax.psum(small_local, ('dp', 'blk'))  40.6 us
    all_to_all x1, starting transfers between devices, per_device(): lax.all_to_all(sent_bins, 'dp', split_axis=0, concat_axis=0, tiled=True)  7.36 us
    while x46, local copies, waits for them, and re-layouts  7.26 us
    all_to_all x1, waiting for transfers between devices, per_device(): lax.all_to_all(sent_wave, 'dp', split_axis=0, concat_axis=0, tiled=True)  5.32 us
    dot_general x2, matrix products, pass_group(): jnp.dot(cols_two, conv_two, preferred_element_type=jnp.float32) + bias_two  4.2 us
    dot_general x1, matrix products, per_device(): lax.dot_general(cols_all, dz_all, (((0,), (0,)), ((), ())), preferred_ele...  4.2 us
    all_to_all x1, waiting for transfers between devices, per_device(): lax.all_to_all(sent_bins, 'dp', split_axis=0, concat_axis=0, tiled=True)  3.87 us
  transfers between devices with their start and end apart: 4, of which 3 were waited for; matrix products, arithmetic and copies ran while one was open for 2% of the time, Pallas kernels for 0%

commit v1 on v0

--- a/solution.py
+++ b/solution.py
@@ -153,7 +153,7 @@
     )
     whole = lax.psum(term, "blk")
     share = lax.psum_scatter(whole, "dp", scatter_dimension=0, tiled=True)
-    small_total = lax.psum(small_local, ("dp", "blk"))
+    small_total = lax.psum(lax.psum(small_local, "blk"), "dp")
     return (share, small_total)
 
 

time: 193 us -> 220 us (1.14)
  blocking collectives: 40.6 us -> 67.2 us
    psum x1 -> x2, blocking collectives: 40.6 us -> 67.2 us  [per_device(): small_total = lax.psum(lax.psum(small_local, 'blk'), 'dp')]
where the time goes in v1:
time: 220 us; the launch traced here: 219 us
  waiting for transfers between devices  72.8 us (33%)
  blocking collectives  67.2 us (31%)
  local copies, waits for them, and re-layouts  25.6 us (12%)
  other arithmetic  16.9 us (8%)
  between operations  14.1 us (6%)
  starting transfers between devices  10.9 us (5%)
  matrix products  10.8 us (5%)
    psum x2, blocking collectives, per_device(): small_total = lax.psum(lax.psum(small_local, 'blk'), 'dp')  67.2 us
    reduce_scatter x1, waiting for transfers between devices, per_device(): share = lax.psum_scatter(whole, 'dp', scatter_dimension=0, tiled=True)  63.6 us
    all_to_all x1, starting transfers between devices, per_device(): lax.all_to_all(sent_bins, 'dp', split_axis=0, concat_axis=0, tiled=True)  7.36 us
    while x46, local copies, waits for them, and re-layouts  7.26 us
    all_to_all x1, waiting for transfers between devices, per_device(): lax.all_to_all(sent_wave, 'dp', split_axis=0, concat_axis=0, tiled=True)  5.32 us
  transfers between devices with their start and end apart: 4, of which 3 were waited for; matrix products, arithmetic and copies ran while one was open for 2% of the time, Pallas kernels for 0%

profile of v1, /device:TPU:0, one launch (start us, length us, event | category | flops | bytes accessed | tf_op | source)
XLA Modules:
  0.0 219.0 jit_solution(13434741510211362902)
XLA Ops:
  7.9 1.3 gather_fusion.1
  9.9 7.4 %all-to-all-start.1 = ((s32[16,1,1]{2,1,0:T(1,128)}), s32[16,1,1]{2,1,0:T(1,128)S(1)}, u32[]{:S(2)}, u32[]{:S(2)}) async-start(s32[16,1,1]{2,1,0:T(1,128)} %copy.29), calls=%async_computation.1 | async-start | bytes 16384 | tf_op jit(solution)/shard_map/all_to_all | solution.py:119
  19.7 3.9 %all-to-all-done.1 = s32[16,1,1]{2,1,0:T(1,128)S(1)} async-done(((s32[16,1,1]{2,1,0:T(1,128)}), s32[16,1,1]{2,1,0:T(1,128)S(1)}, u32[]{:S(2)}, u32[]{:S(2)}) %all-to-all-start.1) | async-done | bytes 96 | tf_op jit(solution)/shard_map/all_to_all | solution.py:119
  23.6 3.5 %all-to-all-start = ((bf16[16,2,165]{2,1,0:T(2,128)(2,1)}), bf16[16,2,165]{2,1,0:T(2,128)(2,1)S(1)}, u32[]{:S(2)}, u32[]{:S(2)}) async-start(bf16[16,2,165]{2,1,0:T(2,128)(2,1)} %reshape.260), calls=%async_computation | async-start | bytes 32768 | tf_op jit(solution)/shard_map/all_to_all | solution.py:118
  28.2 5.3 %all-to-all-done = bf16[16,2,165]{2,1,0:T(2,128)(2,1)S(1)} async-done(((bf16[16,2,165]{2,1,0:T(2,128)(2,1)}), bf16[16,2,165]{2,1,0:T(2,128)(2,1)S(1)}, u32[]{:S(2)}, u32[]{:S(2)}) %all-to-all-start) | async-done | bytes 10592 | tf_op jit(solution)/shard_map/all_to_all | solution.py:118
  34.2 41.1 %while.17 = (s32[]{:T(128)}, f32[16,512]{1,0:T(8,128)}, bf16[2,256,1536]{2,1,0:T(8,128)(2,1)}, bf16[2,256,512]{2,1,0:T(8,128)(2,1)}, bf16[2,8,330]{2,1,0:T(8,128...) while((s32[]{:T(128)}, f32[16,512]{1,0:T(8,128)}, ...), condition=%wide.region_15.16_spmd.clone, body=%wide.region_0.15_spmd.clone.sunk | while | flops 835685888 | bytes 56027588 | solution.py:148
  39.0 2.1 fusion.59
  43.3 0.9 maximum_dynamic-update-slice_fusion.2
  46.7 1.6 copy.42
  48.6 1.7 reshape.273
  50.4 1.5 pad_add_fusion.2
  52.0 1.1 multiply_reduce_fusion.15
  59.2 2.1 fusion.59
  63.5 0.9 maximum_dynamic-update-slice_fusion.2
  66.9 1.6 copy.42
  68.8 1.7 reshape.273
  70.6 1.5 pad_add_fusion.2
  72.2 1.1 multiply_reduce_fusion.15
  74.0 1.4 select_add_fusion.2
  75.4 4.2 %convolution_bitcast_fusion = f32[1536,512]{1,0:T(8,128)} fusion(bf16[2,256,1536]{2,1,0:T(8,128)(2,1)} %get-tuple-element.190, bf16[2,256,512]{2,1,0:T(8,128)(2,1)} %get-tuple-element.191), kind=kOutput, calls=%fused_computation.65 | convolution fusion | flops 805306368 | bytes 5242880 | tf_op jit(solution)/shard_map/dot_general | solution.py:151
  79.6 63.6 %reduce-scatter.2.cloned.1.call-done = f32[96,512]{1,0:T(8,128)} async-done(((f32[1536,512]{1,0:T(8,128)}), f32[96,512]{1,0:T(8,128)}) %reduce-scatter.2.cloned.1.call-update) | async-done | bytes 196624 | tf_op jit(solution)/shard_map/reduce_scatter | solution.py:155
  143.3 9.0 %psum.22 = f32[16,512]{1,0:T(8,128)S(1)} all-reduce(f32[16,512]{1,0:T(8,128)} %get-tuple-element.192), channel_id=1, replica_groups=mesh['dp'=16,'blk'=2] {'blk'}, use_global_device_ids=true, to_apply=%region_18.19 | all-reduce | flops 8192 | bytes 65536 | tf_op jit(solution)/shard_map/psum | solution.py:156
  152.3 58.2 %psum.23 = f32[16,512]{1,0:T(8,128)} all-reduce(f32[16,512]{1,0:T(8,128)S(1)} %psum.22), channel_id=1, replica_groups=mesh['dp'=16,'blk'=2] {'dp'}, use_global_device_ids=true, to_apply=%region_19.20 | all-reduce | flops 8192 | bytes 65536 | tf_op jit(solution)/shard_map/psum | solution.py:156
  210.5 1.6 copy.58
  (144 shorter events, 27.0 us)
Async XLA Ops:
  7.2 10.1 %copy-start = (bf16[16,330]{1,0:T(8,128)(2,1)S(1)}, bf16[16,330]{1,0:T(8,128)(2,1)}, u32[]{:S(2)}) copy-start(bf16[16,330]{1,0:T(8,128)(2,1)} %param.14) | copy-start | bytes 31684
  9.9 13.7 %all-to-all-start.1 = ((s32[16,1,1]{2,1,0:T(1,128)}), s32[16,1,1]{2,1,0:T(1,128)S(1)}, u32[]{:S(2)}, u32[]{:S(2)}) async-start(s32[16,1,1]{2,1,0:T(1,128)} %copy.29), calls=%async_computation.1 | async-start | bytes 16384 | tf_op jit(solution)/shard_map/all_to_all | solution.py:119
  23.6 10.0 %all-to-all-start = ((bf16[16,2,165]{2,1,0:T(2,128)(2,1)}), bf16[16,2,165]{2,1,0:T(2,128)(2,1)S(1)}, u32[]{:S(2)}, u32[]{:S(2)}) async-start(bf16[16,2,165]{2,1,0:T(2,128)(2,1)} %reshape.260), calls=%async_computation | async-start | bytes 32768 | tf_op jit(solution)/shard_map/all_to_all | solution.py:118
  27.1 116.2 %reduce-scatter.2.cloned.1.call-start = ((), (), s32[]{:S(2)}) async-start(), calls=%async_computation.3 | async-start | bytes 3342336 | tf_op jit(solution)/shard_map/reduce_scatter | solution.py:155
  34.2 2.3 %copy-start.2 = (bf16[2,8,32,512]{3,2,1,0:T(8,128)(2,1)S(1)}, bf16[2,8,32,512]{3,2,1,0:T(8,128)(2,1)}, u32[]{:S(2)}) copy-start(bf16[2,8,32,512]{3,2,1,0:T(8,128)(2,1)} %get-tuple-element.477) | copy-start | bytes 1572868 | tf_op jit(solution)/shard_map/while
  34.2 2.3 %copy-start.4 = (bf16[10,512]{1,0:T(8,128)(2,1)S(1)}, bf16[10,512]{1,0:T(8,128)(2,1)}, u32[]{:S(2)}) copy-start(bf16[10,512]{1,0:T(8,128)(2,1)} %get-tuple-element.471) | copy-start | bytes 30724 | tf_op jit(solution)/shard_map/while
  34.2 2.3 %copy-start.7 = (f32[512]{0:T(512)S(1)}, f32[512]{0:T(512)}, u32[]{:S(2)}) copy-start(f32[512]{0:T(512)} %get-tuple-element.472) | copy-start | bytes 6148 | tf_op jit(solution)/shard_map/while
  36.5 0.8 copy-start.3
  36.5 0.8 copy-start.5
  39.0 2.3 %copy-start.6 = (f32[512]{0:T(512)S(1)}, f32[512]{0:T(512)}, u32[]{:S(2)}) copy-start(f32[512]{0:T(512)} %get-tuple-element.479) | copy-start | bytes 6148 | tf_op jit(solution)/shard_map/while
  39.0 2.3 %copy-start.8 = (f32[512]{0:T(512)S(1)}, f32[512]{0:T(512)}, u32[]{:S(2)}) copy-start(f32[512]{0:T(512)} %get-tuple-element.480) | copy-start | bytes 6148 | tf_op jit(solution)/shard_map/while
  41.1 1.0 copy-start.9
  42.4 0.8 copy-start.10
  43.3 1.7 copy-start.1
  54.4 2.3 %copy-start.2 = (bf16[2,8,32,512]{3,2,1,0:T(8,128)(2,1)S(1)}, bf16[2,8,32,512]{3,2,1,0:T(8,128)(2,1)}, u32[]{:S(2)}) copy-start(bf16[2,8,32,512]{3,2,1,0:T(8,128)(2,1)} %get-tuple-element.477) | copy-start | bytes 1572868 | tf_op jit(solution)/shard_map/while
  54.4 2.3 %copy-start.4 = (bf16[10,512]{1,0:T(8,128)(2,1)S(1)}, bf16[10,512]{1,0:T(8,128)(2,1)}, u32[]{:S(2)}) copy-start(bf16[10,512]{1,0:T(8,128)(2,1)} %get-tuple-element.471) | copy-start | bytes 30724 | tf_op jit(solution)/shard_map/while
  54.4 2.3 %copy-start.7 = (f32[512]{0:T(512)S(1)}, f32[512]{0:T(512)}, u32[]{:S(2)}) copy-start(f32[512]{0:T(512)} %get-tuple-element.472) | copy-start | bytes 6148 | tf_op jit(solution)/shard_map/while
  56.7 0.8 copy-start.3
  59.2 2.3 %copy-start.6 = (f32[512]{0:T(512)S(1)}, f32[512]{0:T(512)}, u32[]{:S(2)}) copy-start(f32[512]{0:T(512)} %get-tuple-element.479) | copy-start | bytes 6148 | tf_op jit(solution)/shard_map/while
  59.2 2.3 %copy-start.8 = (f32[512]{0:T(512)S(1)}, f32[512]{0:T(512)}, u32[]{:S(2)}) copy-start(f32[512]{0:T(512)} %get-tuple-element.480) | copy-start | bytes 6148 | tf_op jit(solution)/shard_map/while
  61.3 1.0 copy-start.9
  62.6 0.8 copy-start.10
  63.5 1.7 copy-start.1
  79.6 130.9 %all-reduce.5.cloned.1.call-start = ((), (), s32[]{:S(2)}) async-start(), calls=%async_computation.4 | async-start | bytes 393216 | tf_op jit(solution)/shard_map/psum | solution.py:154
  (3 other events, 2.1 us)
Sparse Core Ops, SparseCore 0:
  79.7 63.4 reduce-scatter.1
  145.5 21.3 all-reduce.4
